TPU v7x, 32 devices: a whole 2x2x4 slice. The times are simulated.
32 devices in a mesh: wide: 4 (over y, core), narrow: 8 (over z, x).
Axes of the slice: x: 2, y: 2, z: 4, core: 2. Of those that a mesh axis runs over, the one named last changes fastest.
Arguments:
- leaf_rhs: bfloat16 [64, 1024, 256], P('wide', 'narrow'), may hold values from -6 to 6
- leaf_inv: bfloat16 [64, 256, 256], P('wide', 'narrow'), may hold values from -0.375 to 0.375
- leaf_upd: bfloat16 [64, 5, 256, 256], P('wide', None, 'narrow'), may hold values from -0.0390625 to 0.0390625
- leaf_targets: int32 [64, 5], P('wide'), may hold values from 0 to 2
- sep_rhs: bfloat16 [3, 1024, 256], P(None, 'narrow'), may hold values from -6 to 6
- sep_inv: bfloat16 [3, 256, 256], replicated, may hold values from -0.375 to 0.375
- sep_low: bfloat16 [3, 256, 256], replicated, may hold values from -0.21875 to 0.21875
Outputs:
- leaf_sol: bfloat16 [64, 1024, 256], P('wide', 'narrow')
- sep_sol: bfloat16 [3, 1024, 256], P(None, 'narrow')
All inputs are finite; a program needn't handle non-finite values.
Results may differ from a plain program's by a relative error of at most 0.012.
Values may be sent and summed in bfloat16 or wider, within the bound.
A program may use at most 64 MiB of HBM per device.

v0:
```python
import jax
import jax.numpy as jnp
from jax import lax
from jax.sharding import PartitionSpec as P


def separator_solve(gathered, sep_rhs, sep_inv, sep_low):
    nsep = sep_inv.shape[0]
    solved_list = []
    for row in range(nsep):
        reduced = sep_rhs[row].astype(jnp.float32) - gathered[row]
        for col in range(row):
            reduced = reduced - jnp.dot(
                solved_list[col],
                sep_low[row * (row - 1) // 2 + col],
                preferred_element_type=jnp.float32,
            )
        reduced = reduced.astype(jnp.bfloat16)
        solved_list.append(
            jnp.dot(reduced, sep_inv[row], preferred_element_type=jnp.float32).astype(jnp.bfloat16)
        )
    return jnp.stack(solved_list)


def body(leaf_rhs, leaf_inv, leaf_upd, leaf_targets, sep_rhs, sep_inv, sep_low):
    nsep = sep_inv.shape[0]
    nupd = leaf_upd.shape[1]
    leaves, scenarios, width = leaf_rhs.shape
    onehot = (leaf_targets[:, :, None] == jnp.arange(nsep, dtype=jnp.int32)[None, None, :]).astype(
        jnp.float32
    )
    columns = leaf_rhs
    leaf_sol = jnp.einsum(
        "lcj,lji->lci",
        columns,
        lax.all_gather(leaf_inv, "narrow", axis=1, tiled=True),
        preferred_element_type=jnp.float32,
    ).astype(jnp.bfloat16)
    start_sum = jnp.zeros((nsep, scenarios, width), jnp.float32)
    total = start_sum
    piece = lax.all_gather(leaf_upd, "narrow", axis=2, tiled=True)
    columns = leaf_sol
    for block in range(nupd):
        contrib = jnp.einsum(
            "lcj,lji->lci", columns, piece[:, block], preferred_element_type=jnp.float32
        )
        total = total + jnp.einsum("lci,ls->sci", contrib, onehot[:, block])
    gathered = total
    total = lax.psum(gathered, "wide")
    sep_sol = separator_solve(total, sep_rhs, sep_inv, sep_low)
    return (leaf_sol, sep_sol)


def solution(mesh):
    in_specs = (
        P("wide", "narrow", None),
        P("wide", "narrow", None),
        P("wide", None, "narrow", None),
        P("wide", None),
        P(None, "narrow", None),
        P(),
        P(),
    )
    out_specs = (P("wide", "narrow", None), P(None, "narrow", None))
    return jax.shard_map(body, mesh=mesh, in_specs=in_specs, out_specs=out_specs, check_vma=False)
```

profile of v0, /device:TPU:0, one launch (start us, length us, event | category | flops | bytes accessed | tf_op | source)
XLA Modules:
  0.0 266.1 jit_solution(2337355595048886722)
XLA Ops:
  7.2 0.0 copy-start
  7.2 0.0 all-gather.3.cloned.1.call-start
  7.2 0.7 all-gather.3.cloned.1.call-update
  7.9 0.0 all-gather.5.cloned.1.call-start
  8.0 0.7 all-gather.5.cloned.1.call-update
  8.7 0.0 all-reduce.2.cloned.1.call-start
  8.7 0.7 iota_compare_fusion
  9.4 52.8 %all-gather.3.cloned.1.call-done = bf16[16,256,256]{2,1,0:T(8,128)(2,1)} async-done(((bf16[16,32,256]{2,1,0:T(8,128)(2,1)}), bf16[16,256,256]{2,1,0:T(8,128)(2,1)}) %all-gather.3.cloned.1.call-update) | async-done | bytes 2097168 | tf_op jit(solution)/shard_map/all_gather | solution.py:36
  62.2 2.0 convolution_convert_fusion
  64.2 0.0 copy-start.1
  64.3 149.5 %all-gather.5.cloned.1.call-done = bf16[16,5,256,256]{3,2,1,0:T(8,128)(2,1)} async-done(((bf16[16,5,32,256]{3,2,1,0:T(8,128)(2,1)}), bf16[16,5,256,256]{3,2,1,0:T(8,128)(2,1)}) %all-gather.5.cloned.1.call-update) | async-done | bytes 10485776 | tf_op jit(solution)/shard_map/all_gather | solution.py:41
  213.8 2.2 fusion.3
  216.0 0.7 fusion.11
  216.6 2.7 %fusion.1 = bf16[16,128,256]{2,1,0:T(8,128)(2,1)S(1)} fusion(bf16[16,128,256]{2,1,0:T(8,128)(2,1)S(1)} %convolution_convert_fusion, bf16[16,5,256,256]{3,2,1,0:T(8,128)(2,1)} %all-gather.5.cloned.1.call-done), kind=kOutput, calls=%fused_computation.3 | convolution fusion | flops 268435456 | bytes 4194304 | tf_op jit(solution)/shard_map/lcj,lji->lci/dot_general | solution.py:44
  219.4 0.7 fusion.7
  220.1 0.5 fusion.2
  220.5 0.7 fusion.9
  221.2 0.5 fusion.4
  221.7 0.8 fusion.21
  222.4 0.5 fusion
  222.9 0.0 copy-start.5
  222.9 0.0 copy-start.4
  222.9 0.0 copy-start.3
  222.9 1.5 fusion.24
  224.4 0.0 all-reduce.2.cloned.1.call-update
  224.5 31.5 %all-reduce.2.cloned.1.call-done = f32[3,128,256]{2,0,1:T(4,128)} async-done(((f32[3,128,256]{2,0,1:T(4,128)}), f32[3,128,256]{2,0,1:T(4,128)}) %all-reduce.2.cloned.1.call-update) | async-done | bytes 393232 | tf_op jit(solution)/shard_map/psum | solution.py:49
  256.0 1.9 slice_subtract_fusion.1
  257.9 0.2 convolution_convert_fusion.3
  258.1 0.3 convolution_convert_fusion.2
  258.4 0.2 convolution_subtract_fusion.1
  258.6 0.3 fusion.29
  258.9 0.7 pad_maximum_fusion
  (8 shorter events, 0.0 us)
Async XLA Ops:
  7.2 55.0 %copy-start = (bf16[16,128,256]{2,1,0:T(8,128)(2,1)S(1)}, bf16[16,128,256]{2,1,0:T(8,128)(2,1)}, u32[]{:S(2)}) copy-start(bf16[16,128,256]{2,1,0:T(8,128)(2,1)} %param.7) | copy-start | bytes 3145732
  7.2 55.0 %all-gather.3.cloned.1.call-start = ((), (), s32[]{:S(2)}) async-start(), calls=%async_computation | async-start | bytes 2359296 | tf_op jit(solution)/shard_map/all_gather | solution.py:36
  7.9 205.8 %all-gather.5.cloned.1.call-start = ((), (), s32[]{:S(2)}) async-start(), calls=%async_computation.1 | async-start | bytes 11796480 | tf_op jit(solution)/shard_map/all_gather | solution.py:41
  8.7 247.4 %all-reduce.2.cloned.1.call-start = ((), (), s32[]{:S(2)}) async-start(), calls=%async_computation.2 | async-start | bytes 1048576 | tf_op jit(solution)/shard_map/psum | solution.py:49
  64.2 158.2 %copy-start.1 = (bf16[16,128,256]{2,1,0:T(8,128)(2,1)}, bf16[16,128,256]{2,1,0:T(8,128)(2,1)S(1)}, u32[]{:S(2)}) copy-start(bf16[16,128,256]{2,1,0:T(8,128)(2,1)S(1)} %convolution_convert_fusion) | copy-start | bytes 3145732
  213.8 6.3 %copy-start.2 = (bf16[16,5,256,256]{3,2,1,0:T(8,128)(2,1)S(1)}, bf16[16,5,256,256]{3,2,1,0:T(8,128)(2,1)}, u32[]{:S(2)}) copy-start(bf16[16,5,256,256]{3,2,1,0:T(8,128)(2,1)} %all-gather.5.cloned.1.call-done) | copy-start | bytes 31457284
  222.9 1.6 copy-start.5
  222.9 35.0 %copy-start.4 = (bf16[3,256,256]{2,1,0:T(8,128)(2,1)S(1)}, bf16[3,256,256]{2,1,0:T(8,128)(2,1)}, u32[]{:S(2)}) copy-start(bf16[3,256,256]{2,1,0:T(8,128)(2,1)} %param.12) | copy-start | bytes 1179652
  222.9 35.2 %copy-start.3 = (bf16[3,256,256]{2,1,0:T(8,128)(2,1)S(1)}, bf16[3,256,256]{2,1,0:T(8,128)(2,1)}, u32[]{:S(2)}) copy-start(bf16[3,256,256]{2,1,0:T(8,128)(2,1)} %param.13) | copy-start | bytes 1179652
Sparse Core Ops, SparseCore 0:
  10.2 51.9 all-gather.2
  64.4 149.3 all-gather.4
  224.6 31.4 all-reduce.1
where the time goes:
time: 266 us
  waiting for transfers between devices  235 us (88%)
  between operations  13.9 us (5%)
  matrix products  13.5 us (5%)
  other arithmetic  3.29 us (1%)
    all_gather x1, waiting for transfers between devices, body(): piece = lax.all_gather(leaf_upd, 'narrow', axis=2, tiled=True)  150 us
    all_gather x1, waiting for transfers between devices, body(): lax.all_gather(leaf_inv, 'narrow', axis=1, tiled=True)  52.8 us
    psum x1, waiting for transfers between devices, body(): total = lax.psum(gathered, 'wide')  31.5 us
    dot_general x5, matrix products, body(): jnp.einsum('lcj,lji->lci', columns, piece[:, block], preferred_element_ty...  6.28 us
  transfers between devices with their start and end apart: 3, of which 3 were waited for; matrix products, arithmetic and copies ran while one was open for 1% of the time, Pallas kernels for 0%

commit v1 on v0

--- a/solution.py
+++ b/solution.py
@@ -1,6 +1,10 @@
+import functools
+
 import jax
 import jax.numpy as jnp
 from jax import lax
+from jax.experimental import pallas as pl
+from jax.experimental.pallas import tpu as pltpu
 from jax.sharding import PartitionSpec as P
 
 
@@ -22,7 +26,7 @@
     return jnp.stack(solved_list)
 
 
-def body(leaf_rhs, leaf_inv, leaf_upd, leaf_targets, sep_rhs, sep_inv, sep_low):
+def plain_body(leaf_rhs, leaf_inv, leaf_upd, leaf_targets, sep_rhs, sep_inv, sep_low):
     nsep = sep_inv.shape[0]
     nupd = leaf_upd.shape[1]
     leaves, scenarios, width = leaf_rhs.shape
@@ -51,7 +55,246 @@
     return (leaf_sol, sep_sol)
 
 
+CHUNKS = 4
+NX = 2
+MESH = pl.DeviceIdType.MESH
+
+
+def kernel(nz, rhs_ref, inv_ref, upd_ref, tgt_ref, srhs_ref, sinv_ref, slow_ref, sol_ref, sep_ref,
+           inv_g, sol_s, sol_r, wf, wt, part, r1, q1, r2, q2, r3, gall,
+           zs, zr, xs, xr, as_, ar, s1, v1, s2, v2, s3, v3, s4, v4):
+    nn = nz * NX
+    w, n = lax.axis_index("wide"), lax.axis_index("narrow")
+    core, y = lax.rem(w, 2), w // 2
+    z, x = n // NX, lax.rem(n, NX)
+    leaves, rows, width = inv_ref.shape
+    nupd = upd_ref.shape[1]
+    scen = rhs_ref.shape[1]
+    nsep = sinv_ref.shape[0]
+    per = leaves // CHUNKS
+    slab = nsep * width // 4
+
+    barrier = pltpu.get_barrier_semaphore()
+    for k in range(1, nn):
+        pl.semaphore_signal(barrier, inc=1, device_id={"wide": w, "narrow": lax.rem(n + k, nn)}, device_id_type=MESH)
+    for k in range(1, 4):
+        pl.semaphore_signal(barrier, inc=1, device_id={"wide": lax.rem(w + k, 4), "narrow": n}, device_id_type=MESH)
+    inv_g[n] = inv_ref[...]
+    pl.semaphore_wait(barrier, nn - 1 + 3)
+
+    def send(src, dst, ss, rs, wide, narrow):
+        return pltpu.make_async_remote_copy(
+            src_ref=src, dst_ref=dst, send_sem=ss, recv_sem=rs,
+            device_id={"wide": wide, "narrow": narrow}, device_id_type=MESH)
+
+    def z_copy(c, way, hop, block_z):
+        step = 1 - 2 * way
+        ref = inv_g.at[block_z * NX + x, pl.ds(c * per, per)]
+        return send(ref, ref, zs.at[c, way, hop], zr.at[c, way, hop], w, (z + step) * NX + x)
+
+    def x_copy(c, block_z, side):
+        ref = inv_g.at[block_z * NX + side, pl.ds(c * per, per)]
+        return send(ref, ref, xs.at[c, block_z], xr.at[c, block_z], w, z * NX + 1 - x)
+
+    def can_send(way, hop):
+        if way == 0:
+            return jnp.logical_and(z - hop >= 0, z + 1 <= nz - 1)
+        return jnp.logical_and(z + hop <= nz - 1, z - 1 >= 0)
+
+    def source(way, hop):
+        return z - hop if way == 0 else z + hop
+
+    def has_recv(way, hop):
+        return z - 1 - hop >= 0 if way == 0 else z + 1 + hop <= nz - 1
+
+    for c in range(CHUNKS):
+        for way in range(2):
+            @pl.when(can_send(way, 0))
+            def _(c=c, way=way):
+                z_copy(c, way, 0, source(way, 0)).start()
+        x_copy(c, z, x).start()
+
+    for s in range(nsep):
+        def combine(l, carry, s=s):
+            acc = jnp.zeros((rows, width), jnp.float32)
+            for u in range(nupd):
+                pick = jnp.where(tgt_ref[l, u] == s, 1.0, 0.0).astype(jnp.float32)
+                acc = acc + pick * upd_ref[l, u].astype(jnp.float32)
+            wf[l] = acc
+            return carry
+        lax.fori_loop(0, leaves, combine, 0)
+        wt[pl.ds(s * width, width), :] = wf[...].reshape(leaves * rows, width).T.astype(jnp.bfloat16)
+
+    def relay(c):
+        for hop in range(nz - 1):
+            for way in range(2):
+                @pl.when(has_recv(way, hop))
+                def _(hop=hop, way=way):
+                    step = 1 - 2 * way
+                    block_z = source(way, hop + 1)
+                    ref = inv_g.at[block_z * NX + x, pl.ds(c * per, per)]
+                    send(ref, ref, zs.at[c, way, hop], zr.at[c, way, hop], w, (z - step) * NX + x).wait_recv()
+                    x_copy(c, block_z, x).start()
+                    if hop + 1 < nz - 1:
+                        @pl.when(can_send(way, hop + 1))
+                        def _():
+                            z_copy(c, way, hop + 1, block_z).start()
+
+    def a_copy(c, peer, owner, sem):
+        return send(sol_s.at[peer, pl.ds(c * per, per)], sol_r.at[owner, pl.ds(c * per, per)],
+                    as_.at[c, sem], ar.at[c, sem], w, peer)
+
+    def solve(c):
+        for b in range(nz):
+            x_copy(c, b, 1 - x).wait_recv()
+
+        def one(i, carry):
+            l = c * per + i
+            full = inv_g[:, l].reshape(nn * rows, width)
+            out = jnp.dot(rhs_ref[l], full, preferred_element_type=jnp.float32)
+            sol_ref[l] = out.astype(jnp.bfloat16)
+            sol_s[:, l] = out.T.astype(jnp.bfloat16).reshape(nn, rows, scen)
+            return carry
+        lax.fori_loop(0, per, one, 0)
+        for k in range(1, nn):
+            a_copy(c, lax.rem(n + k, nn), n, k).start()
+
+    relay(0)
+    for c in range(CHUNKS):
+        if c + 1 < CHUNKS:
+            relay(c + 1)
+        solve(c)
+    sol_r[n] = sol_s[n]
+
+    mate, across = w + 1 - 2 * core, lax.rem(w + 2, 4)
+
+    def c1(m, k):
+        return send(part.at[m, 1 - core], r1.at[m], s1.at[k], v1.at[k], mate, n)
+
+    def c2(m, k):
+        return send(q1.at[m, 1 - y], r2.at[m], s2.at[k], v2.at[k], across, n)
+
+    def c3(m, k):
+        return send(q2.at[m], r3.at[n], s3.at[k], v3.at[k], w, m)
+
+    def multiply(k):
+        m = lax.rem(n + nn - k, nn)
+        if k:
+            for c in range(CHUNKS):
+                a_copy(c, m, m, k).wait_recv()
+        block = sol_r[m].reshape(leaves * rows, scen)
+        out = jnp.dot(wt[...], block, preferred_element_type=jnp.float32).astype(jnp.bfloat16)
+        for a in range(2):
+            for b in range(2):
+                q = b * 2 + a
+                part[m, a, b] = out[q * slab:(q + 1) * slab]
+        c1(m, k).start()
+
+    def add_core(k):
+        m = lax.rem(n + nn - k, nn)
+        c1(m, k).wait_recv()
+        q1[m] = (part[m, core].astype(jnp.float32) + r1[m].astype(jnp.float32)).astype(jnp.bfloat16)
+        c2(m, k).start()
+
+    def add_across(k):
+        m = lax.rem(n + nn - k, nn)
+        c2(m, k).wait_recv()
+        q2[m] = (q1[m, y].astype(jnp.float32) + r2[m].astype(jnp.float32)).astype(jnp.bfloat16)
+        if k:
+            c3(m, k).start()
+
+    order = list(range(1, nn)) + [0]
+    for i in range(nn + 2):
+        if i < nn:
+            multiply(order[i])
+        if 0 <= i - 1 < nn:
+            add_core(order[i - 1])
+        if 0 <= i - 2 < nn:
+            add_across(order[i - 2])
+
+    total = q2[n].astype(jnp.float32)
+    for k in range(1, nn):
+        m = lax.rem(n + k, nn)
+        send(q2.at[m], r3.at[m], s3.at[k], v3.at[k], w, m).wait_recv()
+        total = total + r3[m].astype(jnp.float32)
+    gall[w] = total.astype(jnp.bfloat16)
+    for k in range(1, 4):
+        send(gall.at[w], gall.at[w], s4.at[k], v4.at[k], lax.rem(w + k, 4), n).start()
+    for k in range(1, 4):
+        m = lax.rem(w + 4 - k, 4)
+        send(gall.at[m], gall.at[m], s4.at[k], v4.at[k], m, n).wait_recv()
+    gathered = gall[...].astype(jnp.float32).reshape(nsep * width, scen)
+    solved = []
+    for s in range(nsep):
+        reduced = srhs_ref[s].astype(jnp.float32) - gathered[s * width:(s + 1) * width].T
+        for t in range(s):
+            reduced = reduced - jnp.dot(solved[t], slow_ref[s * (s - 1) // 2 + t], preferred_element_type=jnp.float32)
+        solved.append(jnp.dot(reduced.astype(jnp.bfloat16), sinv_ref[s], preferred_element_type=jnp.float32).astype(jnp.bfloat16))
+        sep_ref[s] = solved[s]
+
+    for c in range(CHUNKS):
+        for way in range(2):
+            for hop in range(nz - 1):
+                @pl.when(can_send(way, hop))
+                def _(c=c, way=way, hop=hop):
+                    z_copy(c, way, hop, source(way, hop)).wait_send()
+        for b in range(nz):
+            x_copy(c, b, x).wait_send()
+        for k in range(1, nn):
+            a_copy(c, lax.rem(n + k, nn), n, k).wait_send()
+    for k in range(nn):
+        m = lax.rem(n + nn - k, nn)
+        c1(m, k).wait_send()
+        c2(m, k).wait_send()
+        if k:
+            c3(m, k).wait_send()
+    for k in range(1, 4):
+        send(gall.at[w], gall.at[w], s4.at[k], v4.at[k], lax.rem(w + k, 4), n).wait_send()
+
+
+def fused_body(nn, leaf_rhs, leaf_inv, leaf_upd, leaf_targets, sep_rhs, sep_inv, sep_low):
+    leaves, scen, width = leaf_rhs.shape
+    rows = leaf_inv.shape[1]
+    nsep = sep_inv.shape[0]
+    nz = nn // NX
+    slab = nsep * width // 4
+    bf = jnp.bfloat16
+    vmem = pl.BlockSpec(memory_space=pltpu.VMEM)
+    dma = pltpu.SemaphoreType.DMA
+    return pl.pallas_call(
+        functools.partial(kernel, nz),
+        out_shape=(jax.ShapeDtypeStruct(leaf_rhs.shape, bf), jax.ShapeDtypeStruct(sep_rhs.shape, bf)),
+        in_specs=[vmem, vmem, vmem, pl.BlockSpec(memory_space=pltpu.SMEM), vmem, vmem, vmem],
+        out_specs=(vmem, vmem),
+        scratch_shapes=[
+            pltpu.VMEM((nn, leaves, rows, width), bf),
+            pltpu.VMEM((nn, leaves, rows, scen), bf),
+            pltpu.VMEM((nn, leaves, rows, scen), bf),
+            pltpu.VMEM((leaves, rows, width), jnp.float32),
+            pltpu.VMEM((nsep * width, leaves * rows), bf),
+            pltpu.VMEM((nn, 2, 2, slab, scen), bf),
+            pltpu.VMEM((nn, 2, slab, scen), bf),
+            pltpu.VMEM((nn, 2, slab, scen), bf),
+            pltpu.VMEM((nn, slab, scen), bf),
+            pltpu.VMEM((nn, slab, scen), bf),
+            pltpu.VMEM((nn, slab, scen), bf),
+            pltpu.VMEM((4, slab, scen), bf),
+            dma((CHUNKS, 2, nz)), dma((CHUNKS, 2, nz)),
+            dma((CHUNKS, nz)), dma((CHUNKS, nz)),
+            dma((CHUNKS, nn)), dma((CHUNKS, nn)),
+            dma((nn,)), dma((nn,)), dma((nn,)), dma((nn,)), dma((nn,)), dma((nn,)),
+            dma((4,)), dma((4,)),
+        ],
+        compiler_params=pltpu.CompilerParams(
+            collective_id=0, has_side_effects=True, vmem_limit_bytes=40 * 2**20),
+    )(leaf_rhs, leaf_inv, leaf_upd, leaf_targets, sep_rhs, sep_inv, sep_low)
+
+
 def solution(mesh):
+    if mesh.shape["wide"] == 4 and mesh.shape["narrow"] == 8:
+        body = functools.partial(fused_body, mesh.shape["narrow"])
+    else:
+        body = plain_body
     in_specs = (
         P("wide", "narrow", None),
         P("wide", "narrow", None),

time: 266 us -> 82.6 us (0.31)
  waiting for transfers between devices: 235 us -> 0 us
  Pallas kernels: 0 us -> 72.8 us
  matrix products: 13.5 us -> 0 us
  between operations: 13.9 us -> 0.64 us
  local copies, waits for them, and re-layouts: 0.05 us -> 8.82 us
  other arithmetic: 3.29 us -> 0 us
    all_gather x2 -> x0, waiting for transfers between devices: 202 us -> none  [the longest x1 150 us: body(): piece = lax.all_gather(leaf_upd, 'narrow', axis=2, tiled=True)]
    pallas_call x0 -> x1, Pallas kernels: none -> 72.8 us  [fused_body(): pl.pallas_call(functools.partial(kernel, nz), out_shape=(jax.ShapeDtypeSt...]
    psum x1 -> x0, waiting for transfers between devices: 31.5 us -> none  [body(): total = lax.psum(gathered, 'wide')]
    dot_general x15 -> x0, matrix products: 13.5 us -> none  [the longest x5 6.28 us: body(): jnp.einsum('lcj,lji->lci', columns, piece[:, block], preferred_element_ty...]
    unnamed x12 -> x15, local copies, waits for them, and re-layouts: 0.04 us -> 8.82 us
  transfers between devices with their start and end apart: 3 -> 0, of which waited for: 3 -> 0; matrix products, arithmetic and copies ran while one was open for 1% -> 0% of each run, Pallas kernels for 0% -> 0%
where the time goes in v1:
time: 82.6 us; the launch traced here: 82.2 us
  Pallas kernels  72.8 us (88%)
  local copies, waits for them, and re-layouts  8.82 us (11%)
    pallas_call x1, Pallas kernels, fused_body(): pl.pallas_call(functools.partial(kernel, nz), out_shape=(jax.ShapeDtypeSt...  72.8 us
    unnamed x15, local copies, waits for them, and re-layouts  8.82 us

profile of v1, /device:TPU:0, one launch (start us, length us, event | category | flops | bytes accessed | tf_op | source)
XLA Modules:
  0.0 82.2 jit_solution(2854451583565546410)
XLA Ops:
  0.6 0.8 copy.9.tgt_ref
  1.4 0.0 copy-start
  1.4 1.3 %copy-done = bf16[16,5,32,256]{3,2,1,0:T(8,128)(2,1)S(1)} copy-done((bf16[16,5,32,256]{3,2,1,0:T(8,128)(2,1)S(1)}, bf16[16,5,32,256]{3,2,1,0:T(8,128)(2,1)}, u32[]{:S(2)}) %copy-start) | copy-done | bytes 1310744
  2.7 0.0 copy-start.1
  2.7 1.2 %copy-done.1 = bf16[16,128,256]{2,1,0:T(8,128)(2,1)S(1)} copy-done((bf16[16,128,256]{2,1,0:T(8,128)(2,1)S(1)}, bf16[16,128,256]{2,1,0:T(8,128)(2,1)}, u32[]{:S(2)}) %copy-start.1) | copy-done | bytes 1048600
  3.9 0.0 copy-start.2
  3.9 1.0 %copy-done.2 = bf16[3,256,256]{2,1,0:T(8,128)(2,1)S(1)} copy-done((bf16[3,256,256]{2,1,0:T(8,128)(2,1)S(1)}, bf16[3,256,256]{2,1,0:T(8,128)(2,1)}, u32[]{:S(2)}) %copy-start.2) | copy-done | bytes 393240
  4.9 0.0 copy-start.3
  4.9 1.0 %copy-done.3 = bf16[3,256,256]{2,1,0:T(8,128)(2,1)S(1)} copy-done((bf16[3,256,256]{2,1,0:T(8,128)(2,1)S(1)}, bf16[3,256,256]{2,1,0:T(8,128)(2,1)}, u32[]{:S(2)}) %copy-start.3) | copy-done | bytes 393240
  5.9 0.0 copy-start.4
  5.9 0.9 %copy-done.4 = bf16[16,32,256]{2,1,0:T(8,128)(2,1)S(1)} copy-done((bf16[16,32,256]{2,1,0:T(8,128)(2,1)S(1)}, bf16[16,32,256]{2,1,0:T(8,128)(2,1)}, u32[]{:S(2)}) %copy-start.4) | copy-done | bytes 262168
  6.9 0.0 copy-start.5
  6.9 0.9 %copy-done.5 = bf16[3,128,256]{2,1,0:T(8,128)(2,1)S(1)} copy-done((bf16[3,128,256]{2,1,0:T(8,128)(2,1)S(1)}, bf16[3,128,256]{2,1,0:T(8,128)(2,1)}, u32[]{:S(2)}) %copy-start.5) | copy-done | bytes 196632
  7.8 72.8 %shard_map.86 = (bf16[16,128,256]{2,1,0:T(8,128)(2,1)S(1)}, bf16[3,128,256]{2,1,0:T(8,128)(2,1)S(1)}) custom-call(bf16[16,128,256]{2,1,0:T(8,128)(2,1)S(1)} %copy-done.1, bf16[16,32,256]{2,1,0:T(8,128)(2,1)S(1)} %copy-done.4, bf16[16,5,32,256]{3,2,1,0:T(8,128)(2,1)S(1)} %copy-done, s32[16,5]{1,0:T(8,128)S(1)} %copy.9.tgt_ref, ...), custom_call_target="tpu_custom_call" | custom-call | tf_op jit(solution)/shard_map/pallas_call | solution.py:264
  80.6 1.0 %copy.12 = bf16[16,128,256]{2,1,0:T(8,128)(2,1)} copy(bf16[16,128,256]{2,1,0:T(8,128)(2,1)S(1)} %get-tuple-element.4) | data formatting | bytes 2097152
  81.6 0.7 copy.13
Async XLA Ops:
  1.4 1.3 %copy-start = (bf16[16,5,32,256]{3,2,1,0:T(8,128)(2,1)S(1)}, bf16[16,5,32,256]{3,2,1,0:T(8,128)(2,1)}, u32[]{:S(2)}) copy-start(bf16[16,5,32,256]{3,2,1,0:T(8,128)(2,1)} %upd_ref.1) | copy-start | bytes 3932164
  2.7 1.2 %copy-start.1 = (bf16[16,128,256]{2,1,0:T(8,128)(2,1)S(1)}, bf16[16,128,256]{2,1,0:T(8,128)(2,1)}, u32[]{:S(2)}) copy-start(bf16[16,128,256]{2,1,0:T(8,128)(2,1)} %rhs_ref.1) | copy-start | bytes 3145732
  3.9 1.0 %copy-start.2 = (bf16[3,256,256]{2,1,0:T(8,128)(2,1)S(1)}, bf16[3,256,256]{2,1,0:T(8,128)(2,1)}, u32[]{:S(2)}) copy-start(bf16[3,256,256]{2,1,0:T(8,128)(2,1)} %sinv_ref.1) | copy-start | bytes 1179652
  4.9 1.0 %copy-start.3 = (bf16[3,256,256]{2,1,0:T(8,128)(2,1)S(1)}, bf16[3,256,256]{2,1,0:T(8,128)(2,1)}, u32[]{:S(2)}) copy-start(bf16[3,256,256]{2,1,0:T(8,128)(2,1)} %slow_ref.1) | copy-start | bytes 1179652
  5.9 0.9 %copy-start.4 = (bf16[16,32,256]{2,1,0:T(8,128)(2,1)S(1)}, bf16[16,32,256]{2,1,0:T(8,128)(2,1)}, u32[]{:S(2)}) copy-start(bf16[16,32,256]{2,1,0:T(8,128)(2,1)} %inv_ref.1) | copy-start | bytes 786436
  6.9 0.9 %copy-start.5 = (bf16[3,128,256]{2,1,0:T(8,128)(2,1)S(1)}, bf16[3,128,256]{2,1,0:T(8,128)(2,1)}, u32[]{:S(2)}) copy-start(bf16[3,128,256]{2,1,0:T(8,128)(2,1)} %srhs_ref.1) | copy-start | bytes 589828

commit v2 on v1

--- a/solution.py
+++ b/solution.py
@@ -60,26 +60,35 @@
 MESH = pl.DeviceIdType.MESH
 
 
-def kernel(nz, rhs_ref, inv_ref, upd_ref, tgt_ref, srhs_ref, sinv_ref, slow_ref, sol_ref, sep_ref,
-           inv_g, sol_s, sol_r, wf, wt, part, r1, q1, r2, q2, r3, gall,
+def kernel(nz, rhs_hbm, inv_ref, upd_hbm, tgt_ref, srhs_hbm, sinv_hbm, slow_hbm, sol_ref, sep_ref,
+           rhs_ref, upd_ref, srhs_ref, sinv_ref, slow_ref, load, inv_g, sol_s, sol_r, wf, wt, part, r1, q1, r2, q2, r3, gall,
            zs, zr, xs, xr, as_, ar, s1, v1, s2, v2, s3, v3, s4, v4):
     nn = nz * NX
     w, n = lax.axis_index("wide"), lax.axis_index("narrow")
     core, y = lax.rem(w, 2), w // 2
     z, x = n // NX, lax.rem(n, NX)
     leaves, rows, width = inv_ref.shape
-    nupd = upd_ref.shape[1]
-    scen = rhs_ref.shape[1]
-    nsep = sinv_ref.shape[0]
+    nupd = upd_hbm.shape[1]
+    scen = rhs_hbm.shape[1]
+    nsep = sinv_hbm.shape[0]
     per = leaves // CHUNKS
     slab = nsep * width // 4
 
+    loads = [
+        pltpu.make_async_copy(src, dst, load.at[i])
+        for i, (src, dst) in enumerate([
+            (inv_ref, inv_g.at[n]), (upd_hbm, upd_ref), (rhs_hbm, rhs_ref),
+            (srhs_hbm, srhs_ref), (sinv_hbm, sinv_ref), (slow_hbm, slow_ref)])
+    ]
+    loads[0].start()
     barrier = pltpu.get_barrier_semaphore()
     for k in range(1, nn):
         pl.semaphore_signal(barrier, inc=1, device_id={"wide": w, "narrow": lax.rem(n + k, nn)}, device_id_type=MESH)
     for k in range(1, 4):
         pl.semaphore_signal(barrier, inc=1, device_id={"wide": lax.rem(w + k, 4), "narrow": n}, device_id_type=MESH)
-    inv_g[n] = inv_ref[...]
+    for copy in loads[1:]:
+        copy.start()
+    loads[0].wait()
     pl.semaphore_wait(barrier, nn - 1 + 3)
 
     def send(src, dst, ss, rs, wide, narrow):
@@ -114,11 +123,12 @@
                 z_copy(c, way, 0, source(way, 0)).start()
         x_copy(c, z, x).start()
 
+    loads[1].wait()
     for s in range(nsep):
         def combine(l, carry, s=s):
             acc = jnp.zeros((rows, width), jnp.float32)
             for u in range(nupd):
-                pick = jnp.where(tgt_ref[l, u] == s, 1.0, 0.0).astype(jnp.float32)
+                pick = jnp.where(tgt_ref[u, l] == s, 1.0, 0.0).astype(jnp.float32)
                 acc = acc + pick * upd_ref[l, u].astype(jnp.float32)
             wf[l] = acc
             return carry
@@ -159,6 +169,7 @@
         for k in range(1, nn):
             a_copy(c, lax.rem(n + k, nn), n, k).start()
 
+    loads[2].wait()
     relay(0)
     for c in range(CHUNKS):
         if c + 1 < CHUNKS:
@@ -203,7 +214,7 @@
         if k:
             c3(m, k).start()
 
-    order = list(range(1, nn)) + [0]
+    order = list(range(nn))
     for i in range(nn + 2):
         if i < nn:
             multiply(order[i])
@@ -224,6 +235,8 @@
         m = lax.rem(w + 4 - k, 4)
         send(gall.at[m], gall.at[m], s4.at[k], v4.at[k], m, n).wait_recv()
     gathered = gall[...].astype(jnp.float32).reshape(nsep * width, scen)
+    for copy in loads[3:]:
+        copy.wait()
     solved = []
     for s in range(nsep):
         reduced = srhs_ref[s].astype(jnp.float32) - gathered[s * width:(s + 1) * width].T
@@ -260,13 +273,16 @@
     slab = nsep * width // 4
     bf = jnp.bfloat16
     vmem = pl.BlockSpec(memory_space=pltpu.VMEM)
+    hbm = pl.BlockSpec(memory_space=pl.ANY)
     dma = pltpu.SemaphoreType.DMA
     return pl.pallas_call(
         functools.partial(kernel, nz),
         out_shape=(jax.ShapeDtypeStruct(leaf_rhs.shape, bf), jax.ShapeDtypeStruct(sep_rhs.shape, bf)),
-        in_specs=[vmem, vmem, vmem, pl.BlockSpec(memory_space=pltpu.SMEM), vmem, vmem, vmem],
+        in_specs=[hbm, hbm, hbm, pl.BlockSpec(memory_space=pltpu.SMEM), hbm, hbm, hbm],
         out_specs=(vmem, vmem),
         scratch_shapes=[
+            pltpu.VMEM(leaf_rhs.shape, bf), pltpu.VMEM(leaf_upd.shape, bf), pltpu.VMEM(sep_rhs.shape, bf),
+            pltpu.VMEM(sep_inv.shape, bf), pltpu.VMEM(sep_low.shape, bf), dma((6,)),
             pltpu.VMEM((nn, leaves, rows, width), bf),
             pltpu.VMEM((nn, leaves, rows, scen), bf),
             pltpu.VMEM((nn, leaves, rows, scen), bf),
@@ -286,8 +302,8 @@
             dma((4,)), dma((4,)),
         ],
         compiler_params=pltpu.CompilerParams(
-            collective_id=0, has_side_effects=True, vmem_limit_bytes=40 * 2**20),
-    )(leaf_rhs, leaf_inv, leaf_upd, leaf_targets, sep_rhs, sep_inv, sep_low)
+            collective_id=0, has_side_effects=True, vmem_limit_bytes=56 * 2**20),
+    )(leaf_rhs, leaf_inv, leaf_upd, leaf_targets.T, sep_rhs, sep_inv, sep_low)
 
 
 def solution(mesh):

time: 82.6 us -> 77.8 us (0.942)
  local copies, waits for them, and re-layouts: 8.82 us -> 3.01 us
  Pallas kernels: 72.8 us -> 73.9 us
    unnamed x15 -> x4, local copies, waits for them, and re-layouts: 8.82 us -> 3.01 us
    pallas_call x1, Pallas kernels: 72.8 us -> 73.9 us  [fused_body(): pl.pallas_call(functools.partial(kernel, nz), out_shape=(jax.ShapeDtypeSt...]
where the time goes in v2:
time: 77.8 us; the launch traced here: 77.6 us
  Pallas kernels  73.9 us (95%)
  local copies, waits for them, and re-layouts  3.01 us (4%)
    pallas_call x1, Pallas kernels, fused_body(): pl.pallas_call(functools.partial(kernel, nz), out_shape=(jax.ShapeDtypeSt...  73.9 us
    unnamed x4, local copies, waits for them, and re-layouts  3.01 us

profile of v2, /device:TPU:0, one launch (start us, length us, event | category | flops | bytes accessed | tf_op | source)
XLA Modules:
  0.0 77.6 jit_solution(1377508393520709433)
XLA Ops:
  0.6 73.9 %shard_map.86 = (bf16[16,128,256]{2,1,0:T(8,128)(2,1)}, bf16[3,128,256]{2,1,0:T(8,128)(2,1)}) custom-call(bf16[16,128,256]{2,1,0:T(8,128)(2,1)} %rhs_hbm.1, bf16[16,32,256]{2,1,0:T(8,128)(2,1)} %inv_ref.1, bf16[16,5,32,256]{3,2,1,0:T(8,128)(2,1)} %upd_hbm.1, s32[5,16]{1,0:T(8,128)} %bitcast.1, bf16[3,128,256]{2,1,0:T(8,128)(2,1)} %srhs_hbm.1, ...), custom_call_target="tpu_custom_call" | custom-call | tf_op jit(solution)/shard_map/pallas_call | solution.py:278
  74.6 0.0 copy-start
  74.6 2.3 %copy.11 = bf16[16,128,256]{2,1,0:T(8,128)(2,1)} copy(bf16[16,128,256]{2,1,0:T(8,128)(2,1)} %get-tuple-element.4) | data formatting | bytes 2097152
  76.9 0.0 copy-done
  76.9 0.7 copy.12
Async XLA Ops:
  74.6 2.3 %copy-start = (bf16[3,128,256]{2,1,0:T(8,128)(2,1)S(1)}, bf16[3,128,256]{2,1,0:T(8,128)(2,1)}, u32[]{:S(2)}) copy-start(bf16[3,128,256]{2,1,0:T(8,128)(2,1)} %get-tuple-element.5) | copy-start | bytes 589828

commit v3 on v2

--- a/solution.py
+++ b/solution.py
@@ -99,11 +99,11 @@
     def z_copy(c, way, hop, block_z):
         step = 1 - 2 * way
         ref = inv_g.at[block_z * NX + x, pl.ds(c * per, per)]
-        return send(ref, ref, zs.at[c, way, hop], zr.at[c, way, hop], w, (z + step) * NX + x)
+        return send(ref, ref, zs.at[way, hop], zr.at[c, way, hop], w, (z + step) * NX + x)
 
     def x_copy(c, block_z, side):
         ref = inv_g.at[block_z * NX + side, pl.ds(c * per, per)]
-        return send(ref, ref, xs.at[c, block_z], xr.at[c, block_z], w, z * NX + 1 - x)
+        return send(ref, ref, xs.at[0], xr.at[c], w, z * NX + 1 - x)
 
     def can_send(way, hop):
         if way == 0:
@@ -135,28 +135,31 @@
         lax.fori_loop(0, leaves, combine, 0)
         wt[pl.ds(s * width, width), :] = wf[...].reshape(leaves * rows, width).T.astype(jnp.bfloat16)
 
-    def relay(c):
-        for hop in range(nz - 1):
-            for way in range(2):
-                @pl.when(has_recv(way, hop))
-                def _(hop=hop, way=way):
-                    step = 1 - 2 * way
-                    block_z = source(way, hop + 1)
-                    ref = inv_g.at[block_z * NX + x, pl.ds(c * per, per)]
-                    send(ref, ref, zs.at[c, way, hop], zr.at[c, way, hop], w, (z - step) * NX + x).wait_recv()
-                    x_copy(c, block_z, x).start()
-                    if hop + 1 < nz - 1:
-                        @pl.when(can_send(way, hop + 1))
-                        def _():
-                            z_copy(c, way, hop + 1, block_z).start()
-
-    def a_copy(c, peer, owner, sem):
-        return send(sol_s.at[peer, pl.ds(c * per, per)], sol_r.at[owner, pl.ds(c * per, per)],
-                    as_.at[c, sem], ar.at[c, sem], w, peer)
+    def relay(c, hop):
+        for way in range(2):
+            @pl.when(has_recv(way, hop))
+            def _(way=way):
+                step = 1 - 2 * way
+                block_z = source(way, hop + 1)
+                ref = inv_g.at[block_z * NX + x, pl.ds(c * per, per)]
+                send(ref, ref, zs.at[way, hop], zr.at[c, way, hop], w, (z - step) * NX + x).wait_recv()
+                if hop + 1 < nz - 1:
+                    @pl.when(can_send(way, hop + 1))
+                    def _():
+                        z_copy(c, way, hop + 1, block_z).start()
+                x_copy(c, block_z, x).start()
+
+    def a_copy(c, peer):
+        return send(sol_s.at[peer, pl.ds(c * per, per)], sol_r.at[n, pl.ds(c * per, per)],
+                    as_.at[0], ar.at[n], w, peer)
+
+    def group(ref, count, ss, rs):
+        part_ref = ref.at[pl.ds(0, count)]
+        return send(part_ref, part_ref, ss, rs, w, z * NX + 1 - x)
 
     def solve(c):
-        for b in range(nz):
-            x_copy(c, b, 1 - x).wait_recv()
+        half = inv_g.at[pl.ds(0, nz), pl.ds(c * per, per)]
+        send(half, half, xs.at[0], xr.at[c], w, z * NX + 1 - x).wait_recv()
 
         def one(i, carry):
             l = c * per + i
@@ -167,73 +170,75 @@
             return carry
         lax.fori_loop(0, per, one, 0)
         for k in range(1, nn):
-            a_copy(c, lax.rem(n + k, nn), n, k).start()
+            a_copy(c, lax.rem(n + k, nn)).start()
 
     loads[2].wait()
-    relay(0)
+    for wave in range(CHUNKS + nz - 1):
+        for hop in range(nz - 1):
+            if 0 <= wave - hop < CHUNKS:
+                relay(wave - hop, hop)
     for c in range(CHUNKS):
-        if c + 1 < CHUNKS:
-            relay(c + 1)
         solve(c)
     sol_r[n] = sol_s[n]
 
     mate, across = w + 1 - 2 * core, lax.rem(w + 2, 4)
 
-    def c1(m, k):
-        return send(part.at[m, 1 - core], r1.at[m], s1.at[k], v1.at[k], mate, n)
-
-    def c2(m, k):
-        return send(q1.at[m, 1 - y], r2.at[m], s2.at[k], v2.at[k], across, n)
-
-    def c3(m, k):
-        return send(q2.at[m], r3.at[n], s3.at[k], v3.at[k], w, m)
+    def pair(k):
+        return pl.ds(lax.rem(n + nn - k, nn), 1)
+
+    def c1(k):
+        return send(part.at[pair(k), 1 - core], r1.at[pair(k)], s1.at[k], v1.at[k], mate, n)
+
+    def c2(k):
+        return send(q1.at[pair(k), 1 - y], r2.at[pair(k)], s2.at[k], v2.at[k], across, n)
+
+    def c3(m):
+        return send(q2.at[m], r3.at[n], s3.at[0], v3.at[0], w, m)
 
     def multiply(k):
-        m = lax.rem(n + nn - k, nn)
-        if k:
-            for c in range(CHUNKS):
-                a_copy(c, m, m, k).wait_recv()
-        block = sol_r[m].reshape(leaves * rows, scen)
-        out = jnp.dot(wt[...], block, preferred_element_type=jnp.float32).astype(jnp.bfloat16)
-        for a in range(2):
-            for b in range(2):
-                q = b * 2 + a
-                part[m, a, b] = out[q * slab:(q + 1) * slab]
-        c1(m, k).start()
+        for m in [lax.rem(n + nn - k, nn)]:
+
+            def arrive(m=m):
+                send(sol_r.at[m], sol_r.at[m], as_.at[0], ar.at[m], w, z * NX + 1 - x).wait_recv()
+            if k:
+                arrive()
+            block = sol_r[m].reshape(leaves * rows, scen)
+            out = jnp.dot(wt[...], block, preferred_element_type=jnp.float32).astype(jnp.bfloat16)
+            for a in range(2):
+                for b in range(2):
+                    q = b * 2 + a
+                    part[m, a, b] = out[q * slab:(q + 1) * slab]
+        c1(k).start()
 
     def add_core(k):
-        m = lax.rem(n + nn - k, nn)
-        c1(m, k).wait_recv()
-        q1[m] = (part[m, core].astype(jnp.float32) + r1[m].astype(jnp.float32)).astype(jnp.bfloat16)
-        c2(m, k).start()
+        c1(k).wait_recv()
+        for m in [lax.rem(n + nn - k, nn)]:
+            q1[m] = (part[m, core].astype(jnp.float32) + r1[m].astype(jnp.float32)).astype(jnp.bfloat16)
+        c2(k).start()
 
     def add_across(k):
-        m = lax.rem(n + nn - k, nn)
-        c2(m, k).wait_recv()
-        q2[m] = (q1[m, y].astype(jnp.float32) + r2[m].astype(jnp.float32)).astype(jnp.bfloat16)
-        if k:
-            c3(m, k).start()
-
-    order = list(range(nn))
+        c2(k).wait_recv()
+        for m in [lax.rem(n + nn - k, nn)]:
+            q2[m] = (q1[m, y].astype(jnp.float32) + r2[m].astype(jnp.float32)).astype(jnp.bfloat16)
+            if k:
+                c3(m).start()
+
     for i in range(nn + 2):
         if i < nn:
-            multiply(order[i])
+            multiply(i)
         if 0 <= i - 1 < nn:
-            add_core(order[i - 1])
+            add_core(i - 1)
         if 0 <= i - 2 < nn:
-            add_across(order[i - 2])
+            add_across(i - 2)
 
     total = q2[n].astype(jnp.float32)
+    group(r3, nn - 1, s3.at[0], v3.at[0]).wait_recv()
     for k in range(1, nn):
-        m = lax.rem(n + k, nn)
-        send(q2.at[m], r3.at[m], s3.at[k], v3.at[k], w, m).wait_recv()
-        total = total + r3[m].astype(jnp.float32)
+        total = total + r3[lax.rem(n + k, nn)].astype(jnp.float32)
     gall[w] = total.astype(jnp.bfloat16)
     for k in range(1, 4):
-        send(gall.at[w], gall.at[w], s4.at[k], v4.at[k], lax.rem(w + k, 4), n).start()
-    for k in range(1, 4):
-        m = lax.rem(w + 4 - k, 4)
-        send(gall.at[m], gall.at[m], s4.at[k], v4.at[k], m, n).wait_recv()
+        send(gall.at[w], gall.at[w], s4.at[0], v4.at[0], lax.rem(w + k, 4), n).start()
+    group(gall, 3, s4.at[0], v4.at[0]).wait_recv()
     gathered = gall[...].astype(jnp.float32).reshape(nsep * width, scen)
     for copy in loads[3:]:
         copy.wait()
@@ -245,24 +250,19 @@
         solved.append(jnp.dot(reduced.astype(jnp.bfloat16), sinv_ref[s], preferred_element_type=jnp.float32).astype(jnp.bfloat16))
         sep_ref[s] = solved[s]
 
-    for c in range(CHUNKS):
-        for way in range(2):
-            for hop in range(nz - 1):
-                @pl.when(can_send(way, hop))
-                def _(c=c, way=way, hop=hop):
-                    z_copy(c, way, hop, source(way, hop)).wait_send()
-        for b in range(nz):
-            x_copy(c, b, x).wait_send()
-        for k in range(1, nn):
-            a_copy(c, lax.rem(n + k, nn), n, k).wait_send()
+    for way in range(2):
+        for hop in range(nz - 1):
+            @pl.when(can_send(way, hop))
+            def _(way=way, hop=hop):
+                ref = inv_g.at[source(way, hop) * NX + x]
+                send(ref, ref, zs.at[way, hop], zr.at[0, way, hop], w, z * NX + 1 - x).wait_send()
+    group(inv_g, nz, xs.at[0], xr.at[0]).wait_send()
+    group(sol_s, nn - 1, as_.at[0], ar.at[0]).wait_send()
     for k in range(nn):
-        m = lax.rem(n + nn - k, nn)
-        c1(m, k).wait_send()
-        c2(m, k).wait_send()
-        if k:
-            c3(m, k).wait_send()
-    for k in range(1, 4):
-        send(gall.at[w], gall.at[w], s4.at[k], v4.at[k], lax.rem(w + k, 4), n).wait_send()
+        c1(k).wait_send()
+        c2(k).wait_send()
+    group(q2, nn - 1, s3.at[0], v3.at[0]).wait_send()
+    group(gall, 3, s4.at[0], v4.at[0]).wait_send()
 
 
 def fused_body(nn, leaf_rhs, leaf_inv, leaf_upd, leaf_targets, sep_rhs, sep_inv, sep_low):
@@ -295,11 +295,11 @@
             pltpu.VMEM((nn, slab, scen), bf),
             pltpu.VMEM((nn, slab, scen), bf),
             pltpu.VMEM((4, slab, scen), bf),
-            dma((CHUNKS, 2, nz)), dma((CHUNKS, 2, nz)),
-            dma((CHUNKS, nz)), dma((CHUNKS, nz)),
-            dma((CHUNKS, nn)), dma((CHUNKS, nn)),
-            dma((nn,)), dma((nn,)), dma((nn,)), dma((nn,)), dma((nn,)), dma((nn,)),
-            dma((4,)), dma((4,)),
+            dma((2, nz)), dma((CHUNKS, 2, nz)),
+            dma((1,)), dma((CHUNKS,)),
+            dma((1,)), dma((nn,)),
+            dma((nn,)), dma((nn,)), dma((nn,)), dma((nn,)), dma((1,)), dma((1,)),
+            dma((1,)), dma((1,)),
         ],
         compiler_params=pltpu.CompilerParams(
             collective_id=0, has_side_effects=True, vmem_limit_bytes=56 * 2**20),

time: 77.8 us -> 72.1 us (0.927)
  Pallas kernels: 73.9 us -> 68.3 us
    pallas_call x1, Pallas kernels: 73.9 us -> 68.3 us  [fused_body(): pl.pallas_call(functools.partial(kernel, nz), out_shape=(jax.ShapeDtypeSt...]
where the time goes in v3:
time: 72.1 us; the launch traced here: 71.9 us
  Pallas kernels  68.3 us (95%)
  local copies, waits for them, and re-layouts  3.01 us (4%)
    pallas_call x1, Pallas kernels, fused_body(): pl.pallas_call(functools.partial(kernel, nz), out_shape=(jax.ShapeDtypeSt...  68.3 us
    unnamed x4, local copies, waits for them, and re-layouts  3.01 us

profile of v3, /device:TPU:0, one launch (start us, length us, event | category | flops | bytes accessed | tf_op | source)
XLA Modules:
  0.0 71.9 jit_solution(4179155689409820468)
XLA Ops:
  0.6 68.3 %shard_map.86 = (bf16[16,128,256]{2,1,0:T(8,128)(2,1)}, bf16[3,128,256]{2,1,0:T(8,128)(2,1)}) custom-call(bf16[16,128,256]{2,1,0:T(8,128)(2,1)} %rhs_hbm.1, bf16[16,32,256]{2,1,0:T(8,128)(2,1)} %inv_ref.1, bf16[16,5,32,256]{3,2,1,0:T(8,128)(2,1)} %upd_hbm.1, s32[5,16]{1,0:T(8,128)} %bitcast.1, bf16[3,128,256]{2,1,0:T(8,128)(2,1)} %srhs_hbm.1, ...), custom_call_target="tpu_custom_call" | custom-call | tf_op jit(solution)/shard_map/pallas_call | solution.py:278
  68.9 0.0 copy-start
  68.9 2.3 %copy.11 = bf16[16,128,256]{2,1,0:T(8,128)(2,1)} copy(bf16[16,128,256]{2,1,0:T(8,128)(2,1)} %get-tuple-element.4) | data formatting | bytes 2097152
  71.3 0.0 copy-done
  71.3 0.7 copy.12
Async XLA Ops:
  68.9 2.3 %copy-start = (bf16[3,128,256]{2,1,0:T(8,128)(2,1)S(1)}, bf16[3,128,256]{2,1,0:T(8,128)(2,1)}, u32[]{:S(2)}) copy-start(bf16[3,128,256]{2,1,0:T(8,128)(2,1)} %get-tuple-element.5) | copy-start | bytes 589828

commit v4 on v3

--- a/solution.py
+++ b/solution.py
@@ -61,7 +61,7 @@
 
 
 def kernel(nz, rhs_hbm, inv_ref, upd_hbm, tgt_ref, srhs_hbm, sinv_hbm, slow_hbm, sol_ref, sep_ref,
-           rhs_ref, upd_ref, srhs_ref, sinv_ref, slow_ref, load, inv_g, sol_s, sol_r, wf, wt, part, r1, q1, r2, q2, r3, gall,
+           rhs_ref, upd_ref, srhs_ref, sinv_ref, slow_ref, load, sol_v, store, inv_g, sol_s, sol_r, wf, wt, part, r1, q1, r2, q2, r3, gall,
            zs, zr, xs, xr, as_, ar, s1, v1, s2, v2, s3, v3, s4, v4):
     nn = nz * NX
     w, n = lax.axis_index("wide"), lax.axis_index("narrow")
@@ -91,6 +91,10 @@
     loads[0].wait()
     pl.semaphore_wait(barrier, nn - 1 + 3)
 
+    def peer(k):
+        zs_of = [z, z + 1 - 2 * lax.rem(z, 2), lax.rem(z + nz // 2, nz), nz - 1 - z]
+        return zs_of[k // NX] * NX + (1 - x if k % NX else x)
+
     def send(src, dst, ss, rs, wide, narrow):
         return pltpu.make_async_remote_copy(
             src_ref=src, dst_ref=dst, send_sem=ss, recv_sem=rs,
@@ -157,6 +161,10 @@
         part_ref = ref.at[pl.ds(0, count)]
         return send(part_ref, part_ref, ss, rs, w, z * NX + 1 - x)
 
+    def keep(c):
+        piece = pl.ds(c * per, per)
+        return pltpu.make_async_copy(sol_v.at[piece], sol_ref.at[piece], store.at[c])
+
     def solve(c):
         half = inv_g.at[pl.ds(0, nz), pl.ds(c * per, per)]
         send(half, half, xs.at[0], xr.at[c], w, z * NX + 1 - x).wait_recv()
@@ -165,12 +173,13 @@
             l = c * per + i
             full = inv_g[:, l].reshape(nn * rows, width)
             out = jnp.dot(rhs_ref[l], full, preferred_element_type=jnp.float32)
-            sol_ref[l] = out.astype(jnp.bfloat16)
+            sol_v[l] = out.astype(jnp.bfloat16)
             sol_s[:, l] = out.T.astype(jnp.bfloat16).reshape(nn, rows, scen)
             return carry
-        lax.fori_loop(0, per, one, 0)
-        for k in range(1, nn):
-            a_copy(c, lax.rem(n + k, nn)).start()
+        lax.fori_loop(0, per, one, 0, unroll=True)
+        for k in (1, 2, 3, 4, 5, 6, 7):
+            a_copy(c, peer(k)).start()
+        keep(c).start()
 
     loads[2].wait()
     for wave in range(CHUNKS + nz - 1):
@@ -184,7 +193,7 @@
     mate, across = w + 1 - 2 * core, lax.rem(w + 2, 4)
 
     def pair(k):
-        return pl.ds(lax.rem(n + nn - k, nn), 1)
+        return pl.ds(peer(k), 1)
 
     def c1(k):
         return send(part.at[pair(k), 1 - core], r1.at[pair(k)], s1.at[k], v1.at[k], mate, n)
@@ -196,7 +205,7 @@
         return send(q2.at[m], r3.at[n], s3.at[0], v3.at[0], w, m)
 
     def multiply(k):
-        for m in [lax.rem(n + nn - k, nn)]:
+        for m in [peer(k)]:
 
             def arrive(m=m):
                 send(sol_r.at[m], sol_r.at[m], as_.at[0], ar.at[m], w, z * NX + 1 - x).wait_recv()
@@ -212,24 +221,25 @@
 
     def add_core(k):
         c1(k).wait_recv()
-        for m in [lax.rem(n + nn - k, nn)]:
+        for m in [peer(k)]:
             q1[m] = (part[m, core].astype(jnp.float32) + r1[m].astype(jnp.float32)).astype(jnp.bfloat16)
         c2(k).start()
 
     def add_across(k):
         c2(k).wait_recv()
-        for m in [lax.rem(n + nn - k, nn)]:
+        for m in [peer(k)]:
             q2[m] = (q1[m, y].astype(jnp.float32) + r2[m].astype(jnp.float32)).astype(jnp.bfloat16)
             if k:
                 c3(m).start()
 
+    order = (0, 1, 2, 3, 4, 5, 6, 7)
     for i in range(nn + 2):
         if i < nn:
-            multiply(i)
+            multiply(order[i])
         if 0 <= i - 1 < nn:
-            add_core(i - 1)
+            add_core(order[i - 1])
         if 0 <= i - 2 < nn:
-            add_across(i - 2)
+            add_across(order[i - 2])
 
     total = q2[n].astype(jnp.float32)
     group(r3, nn - 1, s3.at[0], v3.at[0]).wait_recv()
@@ -257,6 +267,8 @@
                 ref = inv_g.at[source(way, hop) * NX + x]
                 send(ref, ref, zs.at[way, hop], zr.at[0, way, hop], w, z * NX + 1 - x).wait_send()
     group(inv_g, nz, xs.at[0], xr.at[0]).wait_send()
+    for c in range(CHUNKS):
+        keep(c).wait()
     group(sol_s, nn - 1, as_.at[0], ar.at[0]).wait_send()
     for k in range(nn):
         c1(k).wait_send()
@@ -279,10 +291,11 @@
         functools.partial(kernel, nz),
         out_shape=(jax.ShapeDtypeStruct(leaf_rhs.shape, bf), jax.ShapeDtypeStruct(sep_rhs.shape, bf)),
         in_specs=[hbm, hbm, hbm, pl.BlockSpec(memory_space=pltpu.SMEM), hbm, hbm, hbm],
-        out_specs=(vmem, vmem),
+        out_specs=(hbm, vmem),
         scratch_shapes=[
             pltpu.VMEM(leaf_rhs.shape, bf), pltpu.VMEM(leaf_upd.shape, bf), pltpu.VMEM(sep_rhs.shape, bf),
             pltpu.VMEM(sep_inv.shape, bf), pltpu.VMEM(sep_low.shape, bf), dma((6,)),
+            pltpu.VMEM(leaf_rhs.shape, bf), dma((CHUNKS,)),
             pltpu.VMEM((nn, leaves, rows, width), bf),
             pltpu.VMEM((nn, leaves, rows, scen), bf),
             pltpu.VMEM((nn, leaves, rows, scen), bf),

time: 72.1 us -> 69.6 us (0.965)
  Pallas kernels: 68.3 us -> 65.7 us
    pallas_call x1, Pallas kernels: 68.3 us -> 65.7 us  [fused_body(): pl.pallas_call(functools.partial(kernel, nz), out_shape=(jax.ShapeDtypeSt...]
where the time goes in v4:
time: 69.6 us; the launch traced here: 69.4 us
  Pallas kernels  65.7 us (94%)
  local copies, waits for them, and re-layouts  3.01 us (4%)
    pallas_call x1, Pallas kernels, fused_body(): pl.pallas_call(functools.partial(kernel, nz), out_shape=(jax.ShapeDtypeSt...  65.7 us
    unnamed x4, local copies, waits for them, and re-layouts  3.01 us

profile of v4, /device:TPU:0, one launch (start us, length us, event | category | flops | bytes accessed | tf_op | source)
XLA Modules:
  0.0 69.4 jit_solution(14207233813155511481)
XLA Ops:
  0.6 65.7 %shard_map.86 = (bf16[16,128,256]{2,1,0:T(8,128)(2,1)}, bf16[3,128,256]{2,1,0:T(8,128)(2,1)}) custom-call(bf16[16,128,256]{2,1,0:T(8,128)(2,1)} %rhs_hbm.1, bf16[16,32,256]{2,1,0:T(8,128)(2,1)} %inv_ref.1, bf16[16,5,32,256]{3,2,1,0:T(8,128)(2,1)} %upd_hbm.1, s32[5,16]{1,0:T(8,128)} %bitcast.1, bf16[3,128,256]{2,1,0:T(8,128)(2,1)} %srhs_hbm.1, ...), custom_call_target="tpu_custom_call" | custom-call | tf_op jit(solution)/shard_map/pallas_call | solution.py:290
  66.4 0.0 copy-start
  66.4 2.3 %copy.11 = bf16[16,128,256]{2,1,0:T(8,128)(2,1)} copy(bf16[16,128,256]{2,1,0:T(8,128)(2,1)} %get-tuple-element.4) | data formatting | bytes 2097152
  68.7 0.0 copy-done
  68.7 0.7 copy.12
Async XLA Ops:
  66.4 2.3 %copy-start = (bf16[3,128,256]{2,1,0:T(8,128)(2,1)S(1)}, bf16[3,128,256]{2,1,0:T(8,128)(2,1)}, u32[]{:S(2)}) copy-start(bf16[3,128,256]{2,1,0:T(8,128)(2,1)} %get-tuple-element.5) | copy-start | bytes 589828
